TPU v7x, 256 devices: a whole 4x4x8 slice. The times are simulated.
256 devices in a mesh: chan: 32 (over y, z_hi, core), inp: 8 (over x, z_lo).
Axes of the slice: x: 4, y: 4, z: 8 (z_hi: 4, z_lo: 2; z = z_hi * 2 + z_lo), core: 2. Of those that a mesh axis runs over, the one named last changes fastest.
Arguments:
- voltages: bfloat16 [2, 512, 32, 4000], P(None, 'chan', None, 'inp'), may hold values from -200 to 200
Outputs:
- coherence: bfloat16 [2, 32, 4000, 4000], P(None, None, 'chan', 'inp')
All inputs are finite; a program needn't handle non-finite values.
Results may differ from a plain program's by a relative error of at most 0.001.
Values may be sent and summed in bfloat16 or wider, within the bound.
A program may use at most 128 MiB of HBM per device.

v0:
```python
import jax
import jax.numpy as jnp
from jax import lax
from jax.sharding import PartitionSpec as P

SAMPLES = 512


EPSILON = 1e-06


def stack_left(voltage_panel):
    real_part = voltage_panel[0]
    imag_part = voltage_panel[1]
    upper_half = jnp.concatenate([real_part, imag_part], axis=0)
    second = jnp.concatenate([imag_part, -real_part], axis=0)
    return jnp.concatenate([upper_half, second], axis=2)


def mean_power(voltage_panel):
    floated = voltage_panel.astype(jnp.float32)
    return jnp.sum(floated[0] * floated[0] + floated[1] * floated[1], axis=0) / SAMPLES + EPSILON


def flatten_right(voltage_panel):
    return voltage_panel.reshape(
        (2 * voltage_panel.shape[1], voltage_panel.shape[2], voltage_panel.shape[3])
    )


def correlate(left_side, right_flat, left_power, right_power):
    products = jnp.einsum("tca,tcb->cab", left_side, right_flat, preferred_element_type=jnp.float32)
    count_rows = products.shape[1] // 2
    scale_left = lax.rsqrt(left_power)[:, :, None]
    scale_right = lax.rsqrt(right_power)[:, None, :]
    real_part = products[:, :count_rows] / SAMPLES * scale_left * scale_right
    imag_part = products[:, count_rows:] / SAMPLES * scale_left * scale_right
    return jnp.stack([real_part, imag_part]).astype(jnp.bfloat16)


def per_device(voltages):
    columns = lax.all_gather(voltages, "inp", axis=3, tiled=True)
    whole = lax.all_to_all(columns, "chan", split_axis=2, concat_axis=1, tiled=True)
    width = voltages.shape[3]
    own_panel = lax.dynamic_slice_in_dim(whole, lax.axis_index("inp") * width, width, 3)
    result = correlate(
        stack_left(whole), flatten_right(own_panel), mean_power(whole), mean_power(own_panel)
    )
    return lax.all_to_all(result, "chan", split_axis=2, concat_axis=1, tiled=True)


def solution(mesh):
    return jax.shard_map(
        per_device,
        mesh=mesh,
        in_specs=(P(None, "chan", None, "inp"),),
        out_specs=P(None, None, "chan", "inp"),
        check_vma=False,
    )
```

profile of v0, /device:TPU:51, one launch (start us, length us, event | category | flops | bytes accessed | tf_op | source)
XLA Modules:
  0.0 1179.8 jit_solution(16258872064944933039)
XLA Ops:
  6.5 0.0 all-gather.2.cloned.1.call-start
  6.5 5.3 copy.8
  11.9 0.0 all-gather.2.cloned.1.call-update
  11.9 630.5 %all-gather.2.cloned.1.call-done = bf16[2,16,32,4000]{2,1,0,3:T(8,128)(2,1)} async-done(((bf16[2,16,32,500]{2,1,0,3:T(8,128)(2,1)}), bf16[2,16,32,4000]{2,1,0,3:T(8,128)(2,1)}) %all-gather.2.cloned.1.call-update) | async-done | bytes 8192016 | tf_op jit(solution)/shard_map/all_gather | solution.py:42
  642.4 37.9 %copy.9 = bf16[2,16,32,4000]{3,1,0,2:T(8,128)(2,1)} copy(bf16[2,16,32,4000]{2,1,0,3:T(8,128)(2,1)} %all-gather.2.cloned.1.call-done) | data formatting | bytes 16384000 | tf_op jit(solution)/shard_map/all_gather | solution.py:42
  680.3 10.5 all-to-all-start
  690.8 187.9 %all-to-all-done = bf16[2,16,32,4000]{3,1,0,2:T(8,128)(2,1)} async-done(((bf16[2,16,32,4000]{3,1,0,2:T(8,128)(2,1)}), bf16[2,16,32,4000]{3,1,0,2:T(8,128)(2,1)}, u32[]{:S(2)}, u32[]{:S(2)}) %all-to-all-start) | async-done | bytes 8192032 | tf_op jit(solution)/shard_map/all_to_all | solution.py:43
  878.7 7.7 copy.11
  886.4 5.2 fusion.20
  891.6 0.0 copy-start
  891.6 12.9 %bitcast_convert_fusion = f32[2,512,1,4000]{3,1,0,2:T(8,128)} fusion(bf16[2,32,16,1,4000]{4,2,1,0,3:T(8,128)(2,1)} %copy.11), kind=kLoop, calls=%fused_computation.30 | loop fusion | flops 4096000 | bytes 24576000 | tf_op jit(solution)/shard_map/convert_element_type | solution.py:21
  904.5 1.8 fusion.19
  906.3 0.2 fusion.17
  906.5 0.0 copy-done
  906.5 2.5 bitcast_negate_fusion
  909.0 6.4 fusion.9
  915.4 31.2 %fusion.7 = f32[1,8000,500]{1,2,0:T(8,128)} fusion(bf16[1024,500]{1,0:T(8,128)(2,1)S(1)} %bitcast.27, bf16[512,1,4000]{2,0,1:T(8,128)(2,1)} %bitcast_negate_fusion, bf16[512,1,4000]{2,0,1:T(8,128)(2,1)} %bitcast.26, bf16[512,1,4000]{2,0,1:T(8,128)(2,1)} %bitcast.25), kind=kOutput, calls=%fused_computation.8 | convolution fusion | flops 8257536000 | bytes 29312000 | tf_op jit(solution)/shard_map/tca,tcb->cab/dot_general | solution.py:32
  946.6 8.6 fusion.14
  955.2 6.1 pad_maximum_fusion
  961.3 21.5 %copy.12 = bf16[2,1,4000,500]{3,0,1,2:T(2,128)(2,1)} copy(bf16[2,1,4000,500]{2,3,1,0:T(8,128)(2,1)} %pad_maximum_fusion) | data formatting | bytes 16000000 | tf_op jit(solution)/shard_map/stack | solution.py:38
  982.8 184.9 %all_to_all.30 = bf16[2,1,4000,500]{3,0,1,2:T(2,128)(2,1)S(1)} all-to-all(bf16[2,1,4000,500]{3,0,1,2:T(2,128)(2,1)} %copy.12), channel_id=1, replica_groups=mesh['chan'=32,'inp'=8] {'chan'}, dimensions={2} | all-to-all | bytes 16000000 | tf_op jit(solution)/shard_map/all_to_all | solution.py:49
  1167.7 5.2 copy.14
  (2 shorter events, 0.0 us)
Async XLA Ops:
  6.5 635.8 %all-gather.2.cloned.1.call-start = ((), (), s32[]{:S(2)}) async-start(), calls=%async_computation.2 | async-start | bytes 36864000 | tf_op jit(solution)/shard_map/all_gather | solution.py:42
  680.3 198.4 %all-to-all-start = ((bf16[2,16,32,4000]{3,1,0,2:T(8,128)(2,1)}), bf16[2,16,32,4000]{3,1,0,2:T(8,128)(2,1)}, u32[]{:S(2)}, u32[]{:S(2)}) async-start(bf16[2,16,32,4000]{3,1,0,2:T(8,128)(2,1)} %copy.9), calls=%async_computation | async-start | bytes 16777216 | tf_op jit(solution)/shard_map/all_to_all | solution.py:43
  891.6 14.9 %copy-start = (bf16[1,32,16,1,4000]{4,2,0,1,3:T(8,128)(2,1)}, bf16[1,32,16,1,4000]{4,2,0,1,3:T(8,128)(2,1)S(1)}, u32[]{:S(2)}) copy-start(bf16[1,32,16,1,4000]{4,2,0,1,3:T(8,128)(2,1)S(1)} %get-tuple-element.10) | copy-start | bytes 12288004
Sparse Core Ops, SparseCore 0:
  12.0 630.3 all-gather.1
where the time goes:
time: 1180 us
  waiting for transfers between devices  818 us (69%)
  blocking collectives  185 us (16%)
  local copies, waits for them, and re-layouts  82.8 us (7%)
  other arithmetic  38.6 us (3%)
  matrix products  31.2 us (3%)
  between operations  13.4 us (1%)
    all_gather x1, waiting for transfers between devices, per_device(): columns = lax.all_gather(voltages, 'inp', axis=3, tiled=True)  630 us
    all_to_all x1, waiting for transfers between devices, per_device(): lax.all_to_all(columns, 'chan', split_axis=2, concat_axis=1, tiled=True)  188 us
    all_to_all x1, blocking collectives, per_device(): lax.all_to_all(result, 'chan', split_axis=2, concat_axis=1, tiled=True)  185 us
    all_gather x1, local copies, waits for them, and re-layouts, per_device(): columns = lax.all_gather(voltages, 'inp', axis=3, tiled=True)  37.9 us
    dot_general x1, matrix products, correlate(): jnp.einsum('tca,tcb->cab', left_side, right_flat, preferred_element_type=...  31.2 us
  transfers between devices with their start and end apart: 2, of which 2 were waited for; matrix products, arithmetic and copies ran while one was open for 0% of the time, Pallas kernels for 0%

commit v1 on v0

v1 whole, which is shorter than its diff:
```python
import functools

import jax
import jax.numpy as jnp
from jax import lax
from jax.experimental import pallas as pl
from jax.experimental.pallas import tpu as pltpu
from jax.sharding import PartitionSpec as P

SAMPLES = 512
EPSILON = 1e-06
MESH = pl.DeviceIdType.MESH
ROWS = 125
WIDE = 512
HOPS = 4


def kernel(volts, out, gathered, left, left_scale, right_scale, staged,
           in_send, in_recv, ring_send, ring_recv, swap_send, swap_recv, out_send, out_recv):
    chan, inp = lax.axis_index("chan"), lax.axis_index("inp")
    y, z_hi, core = chan // 8, (chan // 2) % 4, chan % 2
    x, z_lo = inp // 2, inp % 2
    z = z_hi * 2 + z_lo

    def device(y_to, x_to):
        return ((y_to * 4 + z_hi) * 2 + core, x_to * 2 + z_lo)

    def along_z(z_to):
        return ((y * 4 + z_to // 2) * 2 + core, x * 2 + z_to % 2)

    def partner(r):
        return (y + r // 4) % 4, (x + r % 4) % 4

    other_core = (chan + 1 - 2 * core, inp)

    barrier = pltpu.get_barrier_semaphore()
    for r in range(1, 16):
        pl.semaphore_signal(barrier, inc=1, device_id=device(*partner(r)), device_id_type=MESH)
    for to in (along_z((z + 1) % 8), along_z((z + 7) % 8), other_core):
        pl.semaphore_signal(barrier, inc=1, device_id=to, device_id_type=MESH)
    pl.semaphore_wait(barrier, 18)

    def in_copy(ch, r):
        y_to, x_to = partner(r)
        src = volts.at[y_to * 4 + x_to, ch]
        dst = gathered.at[ch, x, z_lo, z_hi, core, pl.ds(pl.multiple_of(y * 32, 32), 32)]
        return src, dst, device(y_to, x_to)

    def in_remote(ch, r):
        src, dst, to = in_copy(ch, r)
        return pltpu.make_async_remote_copy(
            src_ref=src, dst_ref=dst, send_sem=in_send.at[ch, r], recv_sem=in_recv.at[ch, r],
            device_id=to, device_id_type=MESH)

    def in_arrival(ch, r):
        y_from, x_from = (y + 4 - r // 4) % 4, (x + 4 - r % 4) % 4
        dst = gathered.at[ch, x_from, z_lo, z_hi, core, pl.ds(pl.multiple_of(y_from * 32, 32), 32)]
        return pltpu.make_async_remote_copy(
            src_ref=dst, dst_ref=dst, send_sem=in_send.at[ch, r], recv_sem=in_recv.at[ch, r],
            device_id=device(y_from, x_from), device_id_type=MESH)

    def in_local(ch):
        src, dst, _ = in_copy(ch, 0)
        return pltpu.make_async_copy(src, dst, in_send.at[ch, 0])

    order = (5, 15, 7, 13, 10, 1, 4, 3, 12, 2, 8, 6, 9, 14, 11)
    for ch in range(2):
        in_local(ch).start()
        for r in order:
            in_remote(ch, r).start()

    def panel(q):
        return (x + y + q % 4) % 4

    def piece(q, source, hop, way):
        whole = gathered.at[q // 4, panel(q), source % 2, source // 2, core]
        if hop < HOPS:
            return whole
        return whole.at[pl.ds(64 * way, 64)]

    def ring_copy(q, hop, way, source):
        ref = piece(q, source, hop, way)
        to = along_z((z + (1 if way == 0 else 7)) % 8)
        return pltpu.make_async_remote_copy(
            src_ref=ref, dst_ref=ref, send_sem=ring_send.at[q, way, hop - 1],
            recv_sem=ring_recv.at[q, way, hop - 1], device_id=to, device_id_type=MESH)

    def ring_out(q, hop, way):
        source = (z + (9 - hop if way == 0 else hop - 1)) % 8
        return ring_copy(q, hop, way, source)

    def ring_in(q, hop, way):
        source = (z + (8 - hop if way == 0 else hop)) % 8
        return ring_copy(q, hop, way, source)

    def send_hop(q, hop):
        for way in range(2):
            if hop > 1:
                ring_in(q, hop - 1, way).wait_recv()
            ring_out(q, hop, way).start()

    def swap(q, own):
        ref = gathered.at[q // 4, panel(q), :, :, own]
        return pltpu.make_async_remote_copy(
            src_ref=ref, dst_ref=ref, send_sem=swap_send.at[q], recv_sem=swap_recv.at[q],
            device_id=other_core, device_id_type=MESH)

    def out_remote(ch, i, j, r):
        return pltpu.make_async_remote_copy(
            src_ref=staged.at[ch, i, j], dst_ref=out.at[:, (y * 4 + x) * 2 + ch],
            send_sem=out_send.at[ch, r], recv_sem=out_recv.at[ch, r],
            device_id=device(i, j), device_id_type=MESH)

    def out_local(ch):
        return pltpu.make_async_copy(
            staged.at[ch, y, x], out.at[:, (y * 4 + x) * 2 + ch], out_send.at[ch, 0])

    def out_arrival(ch, r):
        y_from, x_from = (y + 4 - r // 4) % 4, (x + 4 - r % 4) % 4
        return pltpu.make_async_remote_copy(
            src_ref=staged.at[ch, y, x], dst_ref=out.at[:, (y_from * 4 + x_from) * 2 + ch],
            send_sem=out_send.at[ch, r], recv_sem=out_recv.at[ch, r],
            device_id=device(y_from, x_from), device_id_type=MESH)

    pick_at = ROWS * ((z_hi % 2) * 2 + core)
    row = lax.broadcasted_iota(jnp.int32, (128, WIDE), 0)
    lane = lax.broadcasted_iota(jnp.int32, (128, WIDE), 1)
    pick = jnp.where((lane == row + pick_at) & (row < ROWS), 1.0, 0.0).astype(jnp.bfloat16)

    def prepare(q):
        ch, j = q // 4, panel(q)
        first = gathered[ch, j, z_hi // 2].reshape(32, 2, 16, WIDE)
        turned = jnp.stack([first[:, 1], -first[:, 0]], axis=1)
        upper = lax.dot_general(pick, first.reshape(1024, WIDE), (((1,), (1,)), ((), ())),
                                preferred_element_type=jnp.float32)
        lower = lax.dot_general(pick, turned.reshape(1024, WIDE), (((1,), (1,)), ((), ())),
                                preferred_element_type=jnp.float32)
        left[j, :128] = upper.astype(jnp.bfloat16)
        left[j, 128:] = lower.astype(jnp.bfloat16)
        row_power = jnp.sum(upper * upper, axis=1, keepdims=True) / SAMPLES + EPSILON
        scale = lax.rsqrt(row_power) * (1.0 / SAMPLES)
        left_scale[j, :128] = scale
        left_scale[j, 128:] = scale
        second = gathered[ch, j, z_lo].reshape(1024, WIDE).astype(jnp.float32)
        power = jnp.sum(second * second, axis=0, keepdims=True) / SAMPLES + EPSILON
        right_scale[j] = lax.rsqrt(power)

    def correlate(q):
        prepare(q)
        ch, s = q // 4, q % 4

        def unit(u, _):
            i_at = jnp.where(u <= s, s, u - s - 1)
            j_at = jnp.where(u <= s, u, s)
            i, j = (x + y + i_at) % 4, (x + y + j_at) % 4
            right = gathered[ch, j, z_lo].reshape(1024, WIDE)
            product = jnp.dot(left[i], right, preferred_element_type=jnp.float32)
            product = product * left_scale[i] * right_scale[j]
            staged[ch, i, j] = product.astype(jnp.bfloat16).reshape(2, 128, WIDE)
            r = ((i + 4 - y) % 4) * 4 + (j + 4 - x) % 4

            @pl.when(r == 0)
            def _():
                out_local(ch).start()

            @pl.when(r != 0)
            def _():
                out_remote(ch, i, j, r).start()

            return 0

        lax.fori_loop(0, 2 * s + 1, unit, 0)

    def in_wait(ch):
        in_local(ch).wait()
        for r in order:
            in_arrival(ch, r).wait_recv()

    def step(t, _):
        for ch in range(2):
            @pl.when(t == ch * 4)
            def _(ch=ch):
                in_wait(ch)

        @pl.when(t >= 2)
        def _():
            for way in range(2):
                ring_in(t - 2, HOPS, way).wait_recv()
            swap(t - 2, core).start()

        @pl.when(t < 8)
        def _():
            send_hop(t, 1)

        @pl.when((t >= 1) & (t < 9))
        def _():
            send_hop(t - 1, 3)

        @pl.when(t >= 2)
        def _():
            swap(t - 2, 1 - core).wait_recv()
            correlate(t - 2)

        @pl.when(t < 8)
        def _():
            send_hop(t, 2)

        @pl.when((t >= 1) & (t < 9))
        def _():
            send_hop(t - 1, 4)

        return 0

    lax.fori_loop(0, 10, step, 0)

    def drain_ring(q, _):
        for way in range(2):
            for hop in range(1, HOPS + 1):
                ring_out(q, hop, way).wait_send()
        swap(q, core).wait_send()
        return 0

    lax.fori_loop(0, 8, drain_ring, 0)
    for ch in range(2):
        for r in range(1, 16):
            in_remote(ch, r).wait_send()

    def drain_out(r, _):
        y_to, x_to = partner(r)
        for ch in range(2):
            out_remote(ch, y_to, x_to, r).wait_send()
            out_arrival(ch, r).wait_recv()
        return 0

    lax.fori_loop(1, 16, drain_out, 0)
    for ch in range(2):
        out_local(ch).wait()


def per_device(voltages):
    parts, samples, channels, width = voltages.shape
    volts = jnp.transpose(voltages, (2, 0, 1, 3)).reshape(channels, parts * samples, width)
    volts = jnp.pad(volts, ((0, 0), (0, 0), (0, WIDE - width)))
    volts = volts.reshape(channels // 2, 2, parts * samples, WIDE)
    dma = pltpu.SemaphoreType.DMA
    out = pl.pallas_call(
        kernel,
        name="correlate",
        out_shape=jax.ShapeDtypeStruct((2, channels, 128, WIDE), jnp.bfloat16),
        in_specs=[pl.BlockSpec(memory_space=pltpu.VMEM)],
        out_specs=pl.BlockSpec(memory_space=pl.ANY),
        scratch_shapes=[
            pltpu.VMEM((2, 4, 2, 4, 2, 128, WIDE), jnp.bfloat16),
            pltpu.VMEM((4, 256, 1024), jnp.bfloat16),
            pltpu.VMEM((4, 256, 1), jnp.float32),
            pltpu.VMEM((4, 1, WIDE), jnp.float32),
            pltpu.VMEM((2, 4, 4, 2, 128, WIDE), jnp.bfloat16),
            dma((2, 16)), dma((2, 16)),
            dma((8, 2, HOPS)), dma((8, 2, HOPS)),
            dma((8,)), dma((8,)),
            dma((2, 16)), dma((2, 16)),
        ],
        compiler_params=pltpu.CompilerParams(
            collective_id=0, has_side_effects=True, vmem_limit_bytes=48 << 20),
        cost_estimate=pl.CostEstimate(
            flops=2 * 32 * 256 * 1024 * 512, bytes_accessed=9 << 20, transcendentals=0),
    )(volts)
    return out[:, :, :ROWS, :width]


def solution(mesh):
    return jax.shard_map(
        per_device,
        mesh=mesh,
        in_specs=(P(None, "chan", None, "inp"),),
        out_specs=P(None, None, "chan", "inp"),
        check_vma=False,
    )
```

time: 1180 us -> 213 us (0.18)
  the two profiles are of different devices: /device:TPU:51 before, /device:TPU:45 now
where the time goes in v1:
time: 213 us
  Pallas kernels  199 us (93%)
  local copies, waits for them, and re-layouts  13.3 us (6%)
    pallas_call x1, Pallas kernels, per_device(): pl.pallas_call(kernel, name='correlate', out_shape=jax.ShapeDtypeStruct((...  199 us
    slice x1, local copies, waits for them, and re-layouts, per_device(): return out[:, :, :ROWS, :width]  11.4 us

profile of v1, /device:TPU:45, one launch (start us, length us, event | category | flops | bytes accessed | tf_op | source)
XLA Modules:
  0.0 212.5 jit_solution(399377711068611352)
XLA Ops:
  0.0 1.8 copy.2
  1.8 0.2 pad.4
  2.0 199.2 %correlate.1 = bf16[2,32,128,512]{3,2,1,0:T(8,128)(2,1)} custom-call(bf16[16,2,32,512]{3,2,1,0:T(8,128)(2,1)S(1)} %bitcast.5), custom_call_target="tpu_custom_call" | custom-call | flops 8589934592 | bytes 9437184 | tf_op jit(solution)/shard_map/correlate/pallas_call | solution.py:246
  201.1 11.4 %copy.3 = bf16[2,32,125,500]{3,1,2,0:T(8,128)(2,1)} copy(bf16[2,32,125,500]{3,2,1,0:T(8,128)(2,1)} %bitcast.6) | data formatting | bytes 16000000 | tf_op jit(solution)/shard_map/slice | solution.py:268

commit v2 on v1

--- a/solution.py
+++ b/solution.py
@@ -11,8 +11,30 @@
 EPSILON = 1e-06
 MESH = pl.DeviceIdType.MESH
 ROWS = 125
-WIDE = 512
+COLUMNS = 500
+HALF, PADDED = 250, 256
+WIDE = 2 * PADDED
+PANELS = ("0213", "0132", "1302", "0321")
+EARLY = ("045189a26cdef37b", "015426a8937bfcde")
+LATE = (
+    ("82c3af41be596d70", "c506d287e1bf93a4", "6c2d41af50b7839e", "078539c61be2fad4"),
+    ("c382fa41eb5d7960", "06c52d871eb3af94", "2d6c14af05b3978e", "850793c6b1ead2f4"),
+)
+MIDDLE = (0, 0, 0, 1, 4, 8, 12, 16, 16, 16)
+END = (0, 0, 1, 3, 6, 10, 14, 16, 16, 32)
 HOPS = 4
+
+
+def word(digits, bits):
+    packed = sum(int(digit, 16) << (bits * k) for k, digit in enumerate(digits))
+    return packed - (1 << 32) if packed >= 1 << 31 else packed
+
+
+def choose(at, values):
+    chosen = jnp.int32(values[0])
+    for k, value in enumerate(values[1:], 1):
+        chosen = jnp.where(at == k, jnp.int32(value), chosen)
+    return chosen
 
 
 def kernel(volts, out, gathered, left, left_scale, right_scale, staged,
@@ -69,35 +91,41 @@
         for r in order:
             in_remote(ch, r).start()
 
+    case = (y + 4 - x) % 4
+    panels = choose(case, [word(p, 2) for p in PANELS])
+    orders = [choose(core, [word(o[h:h + 8], 4) for o in EARLY]) for h in (0, 8)]
+    orders += [choose(core * 4 + case, [word(o[h:h + 8], 4) for row in LATE for o in row]) for h in (0, 8)]
+
     def panel(q):
-        return (x + y + q % 4) % 4
-
-    def piece(q, source, hop, way):
-        whole = gathered.at[q // 4, panel(q), source % 2, source // 2, core]
-        if hop < HOPS:
+        return (x + (panels >> (2 * (q % 4))) % 4) % 4
+
+    def piece(q, source, hop, way, part):
+        whole = gathered.at[q // 4, panel(q), source % 2, source // 2, core, pl.ds(64 * part, 64)]
+        if hop < 3:
             return whole
-        return whole.at[pl.ds(64 * way, 64)]
-
-    def ring_copy(q, hop, way, source):
-        ref = piece(q, source, hop, way)
+        half = ((source + 1) // 2 + 1 + way) % 2
+        return whole.at[:, pl.ds(pl.multiple_of(half * PADDED, PADDED), PADDED)]
+
+    def ring_copy(q, hop, way, part, source):
+        ref = piece(q, source, hop, way, part)
         to = along_z((z + (1 if way == 0 else 7)) % 8)
         return pltpu.make_async_remote_copy(
-            src_ref=ref, dst_ref=ref, send_sem=ring_send.at[q, way, hop - 1],
-            recv_sem=ring_recv.at[q, way, hop - 1], device_id=to, device_id_type=MESH)
-
-    def ring_out(q, hop, way):
+            src_ref=ref, dst_ref=ref, send_sem=ring_send.at[q, way, hop - 1, part],
+            recv_sem=ring_recv.at[q, way, hop - 1, part], device_id=to, device_id_type=MESH)
+
+    def ring_out(q, hop, way, part):
         source = (z + (9 - hop if way == 0 else hop - 1)) % 8
-        return ring_copy(q, hop, way, source)
-
-    def ring_in(q, hop, way):
+        return ring_copy(q, hop, way, part, source)
+
+    def ring_in(q, hop, way, part):
         source = (z + (8 - hop if way == 0 else hop)) % 8
-        return ring_copy(q, hop, way, source)
-
-    def send_hop(q, hop):
+        return ring_copy(q, hop, way, part, source)
+
+    def send_hop(q, hop, part):
         for way in range(2):
             if hop > 1:
-                ring_in(q, hop - 1, way).wait_recv()
-            ring_out(q, hop, way).start()
+                ring_in(q, hop - 1, way, part).wait_recv()
+            ring_out(q, hop, way, part).start()
 
     def swap(q, own):
         ref = gathered.at[q // 4, panel(q), :, :, own]
@@ -122,54 +150,60 @@
             send_sem=out_send.at[ch, r], recv_sem=out_recv.at[ch, r],
             device_id=device(y_from, x_from), device_id_type=MESH)
 
-    pick_at = ROWS * ((z_hi % 2) * 2 + core)
-    row = lax.broadcasted_iota(jnp.int32, (128, WIDE), 0)
-    lane = lax.broadcasted_iota(jnp.int32, (128, WIDE), 1)
-    pick = jnp.where((lane == row + pick_at) & (row < ROWS), 1.0, 0.0).astype(jnp.bfloat16)
+    half_at = pl.multiple_of((z_hi % 2) * PADDED, PADDED)
+    row = lax.broadcasted_iota(jnp.int32, (128, PADDED), 0)
+    lane = lax.broadcasted_iota(jnp.int32, (128, PADDED), 1)
+    pick = jnp.where((lane == row + ROWS * core) & (row < ROWS), 1.0, 0.0).astype(jnp.bfloat16)
+
+    in_half = lax.broadcasted_iota(jnp.int32, (256, PADDED), 1) < HALF
 
     def prepare(q):
         ch, j = q // 4, panel(q)
-        first = gathered[ch, j, z_hi // 2].reshape(32, 2, 16, WIDE)
+        first = gathered[ch, j, z_hi // 2, :, :, :, pl.ds(half_at, PADDED)].reshape(32, 2, 16, PADDED)
         turned = jnp.stack([first[:, 1], -first[:, 0]], axis=1)
-        upper = lax.dot_general(pick, first.reshape(1024, WIDE), (((1,), (1,)), ((), ())),
+        upper = lax.dot_general(pick, first.reshape(1024, PADDED), (((1,), (1,)), ((), ())),
                                 preferred_element_type=jnp.float32)
-        lower = lax.dot_general(pick, turned.reshape(1024, WIDE), (((1,), (1,)), ((), ())),
+        lower = lax.dot_general(pick, turned.reshape(1024, PADDED), (((1,), (1,)), ((), ())),
                                 preferred_element_type=jnp.float32)
-        left[j, :128] = upper.astype(jnp.bfloat16)
-        left[j, 128:] = lower.astype(jnp.bfloat16)
+        left[ch, j, :128] = upper.astype(jnp.bfloat16)
+        left[ch, j, 128:] = lower.astype(jnp.bfloat16)
         row_power = jnp.sum(upper * upper, axis=1, keepdims=True) / SAMPLES + EPSILON
         scale = lax.rsqrt(row_power) * (1.0 / SAMPLES)
-        left_scale[j, :128] = scale
-        left_scale[j, 128:] = scale
+        left_scale[ch, j, :128] = scale
+        left_scale[ch, j, 128:] = scale
         second = gathered[ch, j, z_lo].reshape(1024, WIDE).astype(jnp.float32)
         power = jnp.sum(second * second, axis=0, keepdims=True) / SAMPLES + EPSILON
-        right_scale[j] = lax.rsqrt(power)
-
-    def correlate(q):
-        prepare(q)
-        ch, s = q // 4, q % 4
-
-        def unit(u, _):
-            i_at = jnp.where(u <= s, s, u - s - 1)
-            j_at = jnp.where(u <= s, u, s)
-            i, j = (x + y + i_at) % 4, (x + y + j_at) % 4
-            right = gathered[ch, j, z_lo].reshape(1024, WIDE)
-            product = jnp.dot(left[i], right, preferred_element_type=jnp.float32)
-            product = product * left_scale[i] * right_scale[j]
-            staged[ch, i, j] = product.astype(jnp.bfloat16).reshape(2, 128, WIDE)
-            r = ((i + 4 - y) % 4) * 4 + (j + 4 - x) % 4
-
-            @pl.when(r == 0)
-            def _():
-                out_local(ch).start()
-
-            @pl.when(r != 0)
-            def _():
-                out_remote(ch, i, j, r).start()
-
+        right_scale[ch, j] = lax.rsqrt(power)
+
+    def unit(ch, i, j):
+        right = gathered[ch, j, z_lo].reshape(1024, WIDE)
+        product = jnp.dot(left[ch, i], right, preferred_element_type=jnp.float32)
+        product = product * left_scale[ch, i] * right_scale[ch, j]
+        upper = pltpu.roll(product[:, PADDED:], HALF, 1)
+        lower = jnp.where(in_half, product[:, :PADDED], upper).astype(jnp.bfloat16)
+        upper = upper.astype(jnp.bfloat16)
+        for k in range(2):
+            rows = slice(128 * k, 128 * k + ROWS)
+            staged[ch, i, j, k, :, :PADDED] = lower[rows]
+            staged[ch, i, j, k, :, PADDED:] = upper[rows, :COLUMNS - PADDED]
+        r = ((i + 4 - y) % 4) * 4 + (j + 4 - x) % 4
+
+        @pl.when(r == 0)
+        def _():
+            out_local(ch).start()
+
+        @pl.when(r != 0)
+        def _():
+            out_remote(ch, i, j, r).start()
+
+    def units(begin, end):
+        def body(n, _):
+            ch = n // 16
+            at = choose(n // 8, orders) >> (4 * (n % 8))
+            unit(ch, panel((at // 4) % 4), panel(at % 4))
             return 0
 
-        lax.fori_loop(0, 2 * s + 1, unit, 0)
+        lax.fori_loop(begin, end, body, 0)
 
     def in_wait(ch):
         in_local(ch).wait()
@@ -184,31 +218,39 @@
 
         @pl.when(t >= 2)
         def _():
-            for way in range(2):
-                ring_in(t - 2, HOPS, way).wait_recv()
+            for part in range(2):
+                for way in range(2):
+                    ring_in(t - 2, HOPS, way, part).wait_recv()
             swap(t - 2, core).start()
 
-        @pl.when(t < 8)
-        def _():
-            send_hop(t, 1)
-
-        @pl.when((t >= 1) & (t < 9))
-        def _():
-            send_hop(t - 1, 3)
+        for part in range(2):
+            @pl.when(t < 8)
+            def _(part=part):
+                send_hop(t, 1, part)
+
+            @pl.when((t >= 1) & (t < 9))
+            def _(part=part):
+                send_hop(t - 1, 3, part)
+
+        @pl.when(t >= 3)
+        def _():
+            units(choose(t, (0,) + END[:-1]), choose(t, MIDDLE))
+
+        for part in range(2):
+            @pl.when(t < 8)
+            def _(part=part):
+                send_hop(t, 2, part)
+
+            @pl.when((t >= 1) & (t < 9))
+            def _(part=part):
+                send_hop(t - 1, 4, part)
 
         @pl.when(t >= 2)
         def _():
             swap(t - 2, 1 - core).wait_recv()
-            correlate(t - 2)
-
-        @pl.when(t < 8)
-        def _():
-            send_hop(t, 2)
-
-        @pl.when((t >= 1) & (t < 9))
-        def _():
-            send_hop(t - 1, 4)
-
+            prepare(t - 2)
+
+        units(choose(t, MIDDLE), choose(t, END))
         return 0
 
     lax.fori_loop(0, 10, step, 0)
@@ -216,7 +258,8 @@
     def drain_ring(q, _):
         for way in range(2):
             for hop in range(1, HOPS + 1):
-                ring_out(q, hop, way).wait_send()
+                for part in range(2):
+                    ring_out(q, hop, way, part).wait_send()
         swap(q, core).wait_send()
         return 0
 
@@ -240,23 +283,24 @@
 def per_device(voltages):
     parts, samples, channels, width = voltages.shape
     volts = jnp.transpose(voltages, (2, 0, 1, 3)).reshape(channels, parts * samples, width)
-    volts = jnp.pad(volts, ((0, 0), (0, 0), (0, WIDE - width)))
+    gap = jnp.zeros((channels, parts * samples, PADDED - HALF), volts.dtype)
+    volts = jnp.concatenate([volts[:, :, :HALF], gap, volts[:, :, HALF:], gap], axis=2)
     volts = volts.reshape(channels // 2, 2, parts * samples, WIDE)
     dma = pltpu.SemaphoreType.DMA
-    out = pl.pallas_call(
+    return pl.pallas_call(
         kernel,
         name="correlate",
-        out_shape=jax.ShapeDtypeStruct((2, channels, 128, WIDE), jnp.bfloat16),
+        out_shape=jax.ShapeDtypeStruct((2, channels, ROWS, COLUMNS), jnp.bfloat16),
         in_specs=[pl.BlockSpec(memory_space=pltpu.VMEM)],
         out_specs=pl.BlockSpec(memory_space=pl.ANY),
         scratch_shapes=[
             pltpu.VMEM((2, 4, 2, 4, 2, 128, WIDE), jnp.bfloat16),
-            pltpu.VMEM((4, 256, 1024), jnp.bfloat16),
-            pltpu.VMEM((4, 256, 1), jnp.float32),
-            pltpu.VMEM((4, 1, WIDE), jnp.float32),
-            pltpu.VMEM((2, 4, 4, 2, 128, WIDE), jnp.bfloat16),
+            pltpu.VMEM((2, 4, 256, 1024), jnp.bfloat16),
+            pltpu.VMEM((2, 4, 256, 1), jnp.float32),
+            pltpu.VMEM((2, 4, 1, WIDE), jnp.float32),
+            pltpu.VMEM((2, 4, 4, 2, ROWS, COLUMNS), jnp.bfloat16),
             dma((2, 16)), dma((2, 16)),
-            dma((8, 2, HOPS)), dma((8, 2, HOPS)),
+            dma((8, 2, HOPS, 2)), dma((8, 2, HOPS, 2)),
             dma((8,)), dma((8,)),
             dma((2, 16)), dma((2, 16)),
         ],
@@ -265,7 +309,6 @@
         cost_estimate=pl.CostEstimate(
             flops=2 * 32 * 256 * 1024 * 512, bytes_accessed=9 << 20, transcendentals=0),
     )(volts)
-    return out[:, :, :ROWS, :width]
 
 
 def solution(mesh):

time: 213 us -> 185 us (0.87)
  the two profiles are of different devices: /device:TPU:45 before, /device:TPU:51 now
where the time goes in v2:
time: 185 us; the launch traced here: 184 us
  Pallas kernels  170 us (92%)
  local copies, waits for them, and re-layouts  13.6 us (7%)
    pallas_call x1, Pallas kernels, per_device(): pl.pallas_call(kernel, name='correlate', out_shape=jax.ShapeDtypeStruct((...  170 us
    pallas_call x1, local copies, waits for them, and re-layouts, per_device(): pl.pallas_call(kernel, name='correlate', out_shape=jax.ShapeDtypeStruct((...  11.4 us

profile of v2, /device:TPU:51, one launch (start us, length us, event | category | flops | bytes accessed | tf_op | source)
XLA Modules:
  0.0 184.4 jit_solution(13038908354679359037)
XLA Ops:
  0.0 1.6 fusion
  1.6 0.3 copy.5
  1.9 0.3 copy.6
  2.2 0.4 pad_maximum_fusion
  2.6 170.4 %correlate.1 = bf16[2,32,125,500]{3,2,1,0:T(8,128)(2,1)} custom-call(bf16[16,2,32,512]{3,2,1,0:T(8,128)(2,1)S(1)} %bitcast.4), custom_call_target="tpu_custom_call" | custom-call | flops 8589934592 | bytes 9437184 | tf_op jit(solution)/shard_map/correlate/pallas_call | solution.py:290
  173.1 11.4 %copy.4 = bf16[2,32,125,500]{3,1,2,0:T(8,128)(2,1)} copy(bf16[2,32,125,500]{3,2,1,0:T(8,128)(2,1)} %correlate.1) | data formatting | bytes 16000000 | tf_op jit(solution)/shard_map/correlate/pallas_call | solution.py:290
  (1 shorter events, 0.0 us)

commit v3 on v2

--- a/solution.py
+++ b/solution.py
@@ -20,8 +20,8 @@
     ("82c3af41be596d70", "c506d287e1bf93a4", "6c2d41af50b7839e", "078539c61be2fad4"),
     ("c382fa41eb5d7960", "06c52d871eb3af94", "2d6c14af05b3978e", "850793c6b1ead2f4"),
 )
-MIDDLE = (0, 0, 0, 1, 4, 8, 12, 16, 16, 16)
-END = (0, 0, 1, 3, 6, 10, 14, 16, 16, 32)
+MIDDLE = (0, 0, 0, 1, 4, 9, 13, 16, 16, 16)
+END = (0, 0, 1, 4, 7, 11, 15, 16, 16, 32)
 HOPS = 4
 
 
@@ -86,10 +86,12 @@
         return pltpu.make_async_copy(src, dst, in_send.at[ch, 0])
 
     order = (5, 15, 7, 13, 10, 1, 4, 3, 12, 2, 8, 6, 9, 14, 11)
-    for ch in range(2):
+    def in_start(ch):
         in_local(ch).start()
         for r in order:
             in_remote(ch, r).start()
+
+    in_start(0)
 
     case = (y + 4 - x) % 4
     panels = choose(case, [word(p, 2) for p in PANELS])
@@ -232,6 +234,10 @@
             def _(part=part):
                 send_hop(t - 1, 3, part)
 
+        @pl.when(t == 1)
+        def _():
+            in_start(1)
+
         @pl.when(t >= 3)
         def _():
             units(choose(t, (0,) + END[:-1]), choose(t, MIDDLE))
@@ -280,6 +286,10 @@
         out_local(ch).wait()
 
 
+def exchange_rows(by_channel, by_row):
+    by_row[0] = jnp.swapaxes(by_channel[0], 0, 1)
+
+
 def per_device(voltages):
     parts, samples, channels, width = voltages.shape
     volts = jnp.transpose(voltages, (2, 0, 1, 3)).reshape(channels, parts * samples, width)
@@ -287,7 +297,7 @@
     volts = jnp.concatenate([volts[:, :, :HALF], gap, volts[:, :, HALF:], gap], axis=2)
     volts = volts.reshape(channels // 2, 2, parts * samples, WIDE)
     dma = pltpu.SemaphoreType.DMA
-    return pl.pallas_call(
+    out = pl.pallas_call(
         kernel,
         name="correlate",
         out_shape=jax.ShapeDtypeStruct((2, channels, ROWS, COLUMNS), jnp.bfloat16),
@@ -309,6 +319,16 @@
         cost_estimate=pl.CostEstimate(
             flops=2 * 32 * 256 * 1024 * 512, bytes_accessed=9 << 20, transcendentals=0),
     )(volts)
+    out = pl.pallas_call(
+        exchange_rows,
+        name="exchange_rows",
+        grid=(2, 2),
+        in_specs=[pl.BlockSpec((1, channels, 64, COLUMNS), lambda k, i: (k, 0, i, 0))],
+        out_specs=pl.BlockSpec((1, 64, channels, COLUMNS), lambda k, i: (k, i, 0, 0)),
+        out_shape=jax.ShapeDtypeStruct((2, ROWS, channels, COLUMNS), jnp.bfloat16),
+        compiler_params=pltpu.CompilerParams(vmem_limit_bytes=48 << 20),
+    )(out)
+    return jnp.swapaxes(out, 1, 2)
 
 
 def solution(mesh):

time: 185 us -> 179 us (0.968); the launches traced: 184 us -> 176 us
  local copies, waits for them, and re-layouts: 13.6 us -> 2.18 us
  Pallas kernels: 170 us -> 174 us
    pallas_call x1 -> x0, local copies, waits for them, and re-layouts: 11.4 us -> none  [per_device(): pl.pallas_call(kernel, name='correlate', out_shape=jax.ShapeDtypeStruct((...]
    pallas_call x0 -> x1, Pallas kernels: none -> 7.7 us  [per_device(): pl.pallas_call(exchange_rows, name='exchange_rows', grid=(2, 2), in_specs...]
    pallas_call x1, Pallas kernels: 170 us -> 166 us  [per_device(): pl.pallas_call(kernel, name='correlate', out_shape=jax.ShapeDtypeStruct((...]
where the time goes in v3:
time: 179 us; the launch traced here: 176 us
  Pallas kernels  174 us (97%)
  local copies, waits for them, and re-layouts  2.18 us (1%)
    pallas_call x1, Pallas kernels, per_device(): pl.pallas_call(kernel, name='correlate', out_shape=jax.ShapeDtypeStruct((...  166 us
    pallas_call x1, Pallas kernels, per_device(): pl.pallas_call(exchange_rows, name='exchange_rows', grid=(2, 2), in_specs...  7.7 us

profile of v3, /device:TPU:51, one launch (start us, length us, event | category | flops | bytes accessed | tf_op | source)
XLA Modules:
  0.0 176.5 jit_solution(1627945334274422340)
XLA Ops:
  0.0 1.6 fusion
  1.6 0.3 copy.4
  1.9 0.3 copy.5
  2.2 0.4 pad_maximum_fusion
  2.6 166.1 %correlate.1.by_channel = bf16[2,32,125,500]{3,2,1,0:T(8,128)(2,1)} custom-call(bf16[16,2,32,512]{3,2,1,0:T(8,128)(2,1)S(1)} %bitcast.5), custom_call_target="tpu_custom_call" | custom-call | flops 8589934592 | bytes 9437184 | tf_op jit(solution)/shard_map/correlate/pallas_call | solution.py:300
  168.8 7.7 %exchange_rows.1 = bf16[2,125,32,500]{3,2,1,0:T(8,128)(2,1)} custom-call(bf16[2,32,125,500]{3,2,1,0:T(8,128)(2,1)} %correlate.1.by_channel), custom_call_target="tpu_custom_call" | custom-call | tf_op jit(solution)/shard_map/exchange_rows/pallas_call | solution.py:322
  (1 shorter events, 0.0 us)

commit v4 on v3

--- a/solution.py
+++ b/solution.py
@@ -322,9 +322,9 @@
     out = pl.pallas_call(
         exchange_rows,
         name="exchange_rows",
-        grid=(2, 2),
-        in_specs=[pl.BlockSpec((1, channels, 64, COLUMNS), lambda k, i: (k, 0, i, 0))],
-        out_specs=pl.BlockSpec((1, 64, channels, COLUMNS), lambda k, i: (k, i, 0, 0)),
+        grid=(2, 1),
+        in_specs=[pl.BlockSpec((1, channels, ROWS, COLUMNS), lambda k, i: (k, 0, i, 0))],
+        out_specs=pl.BlockSpec((1, ROWS, channels, COLUMNS), lambda k, i: (k, i, 0, 0)),
         out_shape=jax.ShapeDtypeStruct((2, ROWS, channels, COLUMNS), jnp.bfloat16),
         compiler_params=pltpu.CompilerParams(vmem_limit_bytes=48 << 20),
     )(out)

time: 179 us -> 178 us (level)
  no operation moved by 1% of the time
where the time goes in v4:
time: 178 us; the launch traced here: 175 us
  Pallas kernels  173 us (97%)
  local copies, waits for them, and re-layouts  2.18 us (1%)
    pallas_call x1, Pallas kernels, per_device(): pl.pallas_call(kernel, name='correlate', out_shape=jax.ShapeDtypeStruct((...  166 us
    pallas_call x1, Pallas kernels, per_device(): pl.pallas_call(exchange_rows, name='exchange_rows', grid=(2, 1), in_specs...  6.5 us

profile of v4, /device:TPU:51, one launch (start us, length us, event | category | flops | bytes accessed | tf_op | source)
XLA Modules:
  0.0 175.3 jit_solution(17529134031439903277)
XLA Ops:
  0.0 1.6 fusion
  1.6 0.3 copy.4
  1.9 0.3 copy.5
  2.2 0.4 pad_maximum_fusion
  2.6 166.1 %correlate.1.by_channel = bf16[2,32,125,500]{3,2,1,0:T(8,128)(2,1)} custom-call(bf16[16,2,32,512]{3,2,1,0:T(8,128)(2,1)S(1)} %bitcast.5), custom_call_target="tpu_custom_call" | custom-call | flops 8589934592 | bytes 9437184 | tf_op jit(solution)/shard_map/correlate/pallas_call | solution.py:300
  168.8 6.5 %exchange_rows.1 = bf16[2,125,32,500]{3,2,1,0:T(8,128)(2,1)} custom-call(bf16[2,32,125,500]{3,2,1,0:T(8,128)(2,1)} %correlate.1.by_channel), custom_call_target="tpu_custom_call" | custom-call | tf_op jit(solution)/shard_map/exchange_rows/pallas_call | solution.py:322
  (1 shorter events, 0.0 us)
